TPU v7x, 256 devices: a whole 4x4x8 slice. The times are simulated.
256 devices in a mesh: rows: 32 (over x_hi, z, core), cols: 8 (over y, x_lo).
Axes of the slice: x: 4 (x_hi: 2, x_lo: 2; x = x_hi * 2 + x_lo), y: 4, z: 8, core: 2. Of those that a mesh axis runs over, the one named last changes fastest.
Arguments:
- image_tokens: bfloat16 [32, 32, 32, 1024], P('rows', None, 'cols'), may hold values from -1.1953125 to 1.1953125
- cotangent: bfloat16 [32, 32, 32, 1024], P('rows', None, 'cols'), may hold values from -6 to 6
- noise_level: int32 [32], P('rows'), may hold values from 0 to 255
- cond_table: float32 [256, 1024], replicated, may hold values from 0.1 to 1.9
- head_scale: float32 [16], replicated, may hold values from 2 to 12
- w_qkv: bfloat16 [3, 1024, 1024], P(None, 'rows', 'cols'), may hold values from -0.1875 to 0.1875
- w_out: bfloat16 [1024, 1024], P('cols', 'rows'), may hold values from -0.1875 to 0.1875
Outputs:
- output_tokens: bfloat16 [32, 32, 32, 1024], P('rows', None, 'cols')
- grad_tokens: bfloat16 [32, 32, 32, 1024], P('rows', None, 'cols')
- grad_w_qkv: float32 [3, 1024, 1024], P(None, 'rows', 'cols')
- grad_w_out: float32 [1024, 1024], P('cols', 'rows')
All inputs are finite; a program needn't handle non-finite values.
Results may differ from a plain program's by a relative error of at most 0.024.
Values may be sent and summed in bfloat16 or wider, within the bound.
A program may use at most 64 MiB of HBM per device.

v0:
```python
import jax
import jax.numpy as jnp
from jax import lax
from jax.sharding import PartitionSpec as P

HEADS = 16
HDIM = 64


EPS = 1e-06


def block_of(count):
    return max((d for d in range(1, min(count, 512) + 1) if count % d == 0))


def rms_scale(values, gain):
    return values * lax.rsqrt(jnp.mean(values * values, -1, keepdims=True) + EPS) * gain


def unit_rows(query, keys, vals, scale, heads):
    count = query.shape[0]
    q_three = query.reshape(count, heads, -1)
    k_three = keys.reshape(count, heads, -1)
    q_unit = (
        scale[None, :, None]
        * q_three
        / jnp.sqrt(jnp.sum(q_three * q_three, -1, keepdims=True) + EPS)
    )
    k_unit = k_three / jnp.sqrt(jnp.sum(k_three * k_three, -1, keepdims=True) + EPS)
    return (q_unit.reshape(count, -1), k_unit.reshape(count, -1), vals)


def three(arr, heads):
    return arr.reshape(arr.shape[0], heads, -1)


def attend_image(inputs, heads):
    q_bf, k_bf, v_bf, da_bf = inputs
    seq = q_bf.shape[0]
    width = q_bf.shape[1]
    kb = block_of(seq)
    q_three = three(q_bf, heads)
    da_three = three(da_bf, heads)

    def forward_step(step, carry):
        num, den = carry
        k_blk = lax.dynamic_slice_in_dim(k_bf, step * kb, kb, 0)
        v_blk = lax.dynamic_slice_in_dim(v_bf, step * kb, kb, 0)
        scores = jnp.einsum(
            "qhd,khd->hqk", q_three, three(k_blk, heads), preferred_element_type=jnp.float32
        )
        expo = jnp.exp(scores)
        num = num + jnp.einsum(
            "hqk,khd->qhd",
            expo.astype(jnp.bfloat16),
            three(v_blk, heads),
            preferred_element_type=jnp.float32,
        )
        return (num, den + jnp.sum(expo, -1))

    num, den = lax.fori_loop(
        0,
        seq // kb,
        forward_step,
        (
            jnp.zeros((seq, heads, width // heads), jnp.float32),
            jnp.zeros((heads, seq), jnp.float32),
        ),
    )
    inv_den = (1.0 / den).astype(jnp.bfloat16)
    inv_f = inv_den.astype(jnp.float32)
    attn = (num * inv_f.T[:, :, None]).astype(jnp.bfloat16).reshape(seq, width)
    delta = jnp.sum(da_three.astype(jnp.float32) * three(attn, heads).astype(jnp.float32), -1)

    def backward_step(step, carry):
        d_q, key_grads = carry
        k_blk = lax.dynamic_slice_in_dim(k_bf, step * kb, kb, 0)
        v_blk = lax.dynamic_slice_in_dim(v_bf, step * kb, kb, 0)
        scores = jnp.einsum(
            "qhd,khd->hqk", q_three, three(k_blk, heads), preferred_element_type=jnp.float32
        )
        weights = jnp.exp(scores) * inv_f[:, :, None]
        d_prob = jnp.einsum(
            "qhd,khd->hqk", da_three, three(v_blk, heads), preferred_element_type=jnp.float32
        )
        d_score = (weights * (d_prob - delta.T[:, :, None])).astype(jnp.bfloat16)
        w_bf = weights.astype(jnp.bfloat16)
        d_q = d_q + jnp.einsum(
            "hqk,khd->qhd", d_score, three(k_blk, heads), preferred_element_type=jnp.float32
        )
        d_k = jnp.einsum(
            "hqk,qhd->khd", d_score, q_three, preferred_element_type=jnp.float32
        ).reshape(kb, width)
        d_v = jnp.einsum(
            "hqk,qhd->khd", w_bf, da_three, preferred_element_type=jnp.float32
        ).reshape(kb, width)
        part = jnp.concatenate([d_k, d_v], -1)
        return (d_q, lax.dynamic_update_slice_in_dim(key_grads, part, step * kb, 0))

    d_q, key_grads = lax.fori_loop(
        0,
        seq // kb,
        backward_step,
        (
            jnp.zeros((seq, heads, width // heads), jnp.float32),
            jnp.zeros((seq, 2 * width), jnp.float32),
        ),
    )
    return (attn, d_q.reshape(seq, width), key_grads)


def per_device(image_tokens, cotangent, noise_level, cond_table, head_scale, w_qkv, w_out):
    imgs, grid_rows, tile_cols, width = image_tokens.shape
    heads = HEADS // lax.axis_size("cols")
    hw = heads * HDIM
    pick = lax.iota(jnp.int32, cond_table.shape[0])[None, :] == noise_level[:, None]
    gains = jnp.sum(
        jnp.where(pick[:, :, None], cond_table[None], jnp.zeros_like(cond_table)[None]), 1
    )
    gain_grid = gains[:, None, None, :]
    x_tile = image_tokens.astype(jnp.float32)
    normed_tile = rms_scale(x_tile, gain_grid).astype(jnp.bfloat16)
    normed_grid, g_grid = (
        lax.all_gather(normed_tile, "cols", axis=2, tiled=True),
        lax.all_gather(cotangent, "cols", axis=2, tiled=True),
    )
    w_qkv_mine, w_out_mine = (
        lax.all_gather(w_qkv, "rows", axis=1, tiled=True),
        lax.all_gather(w_out, "rows", axis=1, tiled=True),
    )
    grid_cols = normed_grid.shape[2]
    seq = grid_rows * grid_cols
    normed = normed_grid.reshape(imgs * seq, width)
    g_flat = g_grid.reshape(imgs * seq, width)
    scale_mine = lax.dynamic_slice_in_dim(head_scale, lax.axis_index("cols") * heads, heads)
    query = jnp.dot(normed, w_qkv_mine[0], preferred_element_type=jnp.float32)
    keys = jnp.dot(normed, w_qkv_mine[1], preferred_element_type=jnp.float32)
    vals = jnp.dot(normed, w_qkv_mine[2], preferred_element_type=jnp.float32)

    def unit_fn(a, b, c):
        return unit_rows(a, b, c, scale_mine, heads)

    units, unit_back = jax.vjp(unit_fn, query, keys, vals)
    q_bf, k_bf, v_bf = [u.astype(jnp.bfloat16) for u in units]
    dattn = jnp.dot(g_flat, w_out_mine.T, preferred_element_type=jnp.float32).astype(jnp.bfloat16)

    def per_image(arr):
        return arr.reshape(imgs, seq, hw)

    def one_image(inputs):
        return attend_image(inputs, heads)

    attn, d_q, key_grads = lax.map(
        one_image, (per_image(q_bf), per_image(k_bf), per_image(v_bf), per_image(dattn))
    )
    attn = attn.reshape(imgs * seq, hw)
    d_q = d_q.reshape(imgs * seq, hw)
    key_grads = key_grads.reshape(imgs * seq, 2 * hw)
    grads = unit_back((d_q, key_grads[:, :hw], key_grads[:, hw:]))
    gproj = [gr.astype(jnp.bfloat16) for gr in grads]
    local_qkv = jnp.stack(
        [jnp.dot(normed.T, gp, preferred_element_type=jnp.float32) for gp in gproj]
    )
    local_out = jnp.dot(attn.T, g_flat, preferred_element_type=jnp.float32)
    grad_w_qkv, grad_w_out = (
        lax.psum_scatter(
            local_qkv.astype(jnp.bfloat16), "rows", scatter_dimension=1, tiled=True
        ).astype(jnp.float32),
        lax.psum_scatter(
            local_out.astype(jnp.bfloat16), "rows", scatter_dimension=1, tiled=True
        ).astype(jnp.float32),
    )
    out_term = jnp.dot(attn, w_out_mine, preferred_element_type=jnp.float32)
    back_term = jnp.dot(gproj[0], w_qkv_mine[0].T, preferred_element_type=jnp.float32)
    back_term = back_term + jnp.dot(gproj[1], w_qkv_mine[1].T, preferred_element_type=jnp.float32)
    back_term = back_term + jnp.dot(gproj[2], w_qkv_mine[2].T, preferred_element_type=jnp.float32)
    terms = jnp.concatenate([out_term, back_term], -1).reshape(
        imgs, grid_rows, grid_cols, 2 * width
    )
    summed = lax.psum_scatter(
        terms.astype(jnp.bfloat16), "cols", scatter_dimension=2, tiled=True
    ).astype(jnp.float32)
    out_add = summed[..., :width]
    back_add = summed[..., width:]
    output_tokens = (x_tile + out_add).astype(jnp.bfloat16)
    _, norm_back = jax.vjp(lambda val: rms_scale(val, gain_grid), x_tile)
    grad_tokens = (cotangent.astype(jnp.float32) + norm_back(back_add)[0]).astype(jnp.bfloat16)
    return (output_tokens, grad_tokens, grad_w_qkv, grad_w_out)


def solution(mesh):
    return jax.shard_map(
        per_device,
        mesh=mesh,
        in_specs=(
            P("rows", None, "cols", None),
            P("rows", None, "cols", None),
            P("rows"),
            P(),
            P(),
            P(None, "rows", "cols"),
            P("cols", "rows"),
        ),
        out_specs=(
            P("rows", None, "cols", None),
            P("rows", None, "cols", None),
            P(None, "rows", "cols"),
            P("cols", "rows"),
        ),
        check_vma=False,
    )
```

profile of v0, /device:TPU:1, one launch (start us, length us, event | category | flops | bytes accessed | tf_op | source)
XLA Modules:
  0.0 486.4 jit_solution(1130121303792263770)
XLA Ops:
  7.9 1.1 fusion.14
  9.1 1.4 select_reduce_fusion
  10.5 1.8 fusion.16
  13.3 50.1 %all_gather.14 = bf16[128,1024]{0,1:T(8,128)(2,1)} all-gather(bf16[128,32]{0,1:T(8,128)(2,1)S(1)} %copy-done.31), channel_id=1, replica_groups=mesh['rows'=32,'cols'=8] {'rows'}, dimensions={1}, use_global_device_ids=true | all-gather | bytes 270336 | tf_op jit(solution)/shard_map/all_gather | solution.py:130
  63.4 39.1 %all_gather.13 = bf16[3,1024,128]{2,1,0:T(8,128)(2,1)S(1)} all-gather(bf16[3,32,128]{2,1,0:T(8,128)(2,1)S(1)} %copy-done.30), channel_id=1, replica_groups=mesh['rows'=32,'cols'=8] {'rows'}, dimensions={1}, use_global_device_ids=true | all-gather | bytes 811008 | tf_op jit(solution)/shard_map/all_gather | solution.py:129
  105.2 2.8 copy.38
  108.0 2.5 convolution_convert_fusion.6
  110.6 1.8 copy.41
  112.4 1.8 multiply_reduce_fusion.3
  115.9 5.2 %while.46 = (s32[]{:T(128)}, f32[1024,2,64]{0,2,1:T(8,128)S(1)}, f32[2,1024]{1,0:T(2,128)S(1)}, bf16[1024,128]{0,1:T(8,128)(2,1)}, bf16[1024,128]{0,1:T(8,128)(2...) while((s32[]{:T(128)}, f32[1024,2,64]{0,2,1:T(8,128)S(1)}, ...), condition=%wide.region_6.0_spmd.clone, body=%wide.region_4.6_spmd.clone.sunk | while | flops 270796800 | bytes 10518698 | solution.py:62
  122.1 6.2 %all-gather.5.cloned.1.call-done = bf16[1,32,32,1024]{3,1,0,2:T(8,128)(2,1)} async-done(((bf16[1,32,4,1024]{3,1,0,2:T(8,128)(2,1)}), bf16[1,32,32,1024]{3,1,0,2:T(8,128)(2,1)}) %all-gather.5.cloned.1.call-update) | async-done | bytes 2097168 | tf_op jit(solution)/shard_map/all_gather | solution.py:126
  128.3 2.8 copy.43
  131.1 1.5 multiply_reduce_fusion.2
  132.6 1.1 broadcast.119
  133.7 13.0 %while.47 = (s32[]{:T(128)}, f32[1024,2,64]{0,2,1:T(8,128)S(1)}, f32[1024,256]{0,1:T(8,128)}, bf16[1024,128]{0,1:T(8,128)(2,1)}, bf16[1024,2,64]{0,2,1:T(8,128)(...) while((s32[]{:T(128)}, f32[1024,2,64]{0,2,1:T(8,128)S(1)}, ...), condition=%wide.region_9.10_spmd.clone, body=%wide.region_8.9_spmd.clone.sunk | while | flops 677773312 | bytes 31875324 | solution.py:101
  136.2 1.0 multiply_convert_fusion.4
  146.8 3.3 fusion.10
  150.9 1.6 convolution_convert_fusion.1
  152.5 2.0 convolution_convert_fusion
  154.8 1.6 fusion.19
  158.9 1.1 pad_maximum_fusion.1
  160.0 3.6 fusion.22
  164.8 1.4 copy-done.2
  167.8 2.4 pad_maximum_fusion
  170.2 6.6 %copy.45 = bf16[1024,2048]{1,0:T(8,128)(2,1)} copy(bf16[1024,2048]{0,1:T(8,128)(2,1)} %pad_maximum_fusion) | data formatting | bytes 8388608 | tf_op jit(solution)/shard_map/concatenate | solution.py:178
  176.8 6.5 %copy.46 = bf16[1,32,32,2048]{3,1,0,2:T(8,128)(2,1)} copy(bf16[1,32,32,2048]{3,2,1,0:T(8,128)(2,1)} %bitcast.151) | data formatting | bytes 8388608 | tf_op jit(solution)/shard_map/convert_element_type | solution.py:182
  183.3 77.1 %reduce-scatter.8.cloned.1.call-done = bf16[128,32]{0,1:T(8,128)(2,1)} async-done(((bf16[128,1024]{0,1:T(8,128)(2,1)}), bf16[128,32]{0,1:T(8,128)(2,1)}) %reduce-scatter.8.cloned.1.call-update) | async-done | bytes 8208 | tf_op jit(solution)/shard_map/reduce_scatter | solution.py:170
  260.4 1.3 convert_element_type.137
  261.7 115.1 %reduce-scatter.6.cloned.1.call-done = bf16[3,32,128]{2,1,0:T(8,128)(2,1)} async-done(((bf16[3,1024,128]{2,1,0:T(8,128)(2,1)}), bf16[3,32,128]{2,1,0:T(8,128)(2,1)}) %reduce-scatter.6.cloned.1.call-update) | async-done | bytes 24592 | tf_op jit(solution)/shard_map/reduce_scatter | solution.py:167
  376.8 1.4 convert_element_type.135
  378.1 98.3 %reduce-scatter.4.cloned.1.call-done = bf16[1,32,4,2048]{3,1,0,2:T(8,128)(2,1)} async-done(((bf16[1,32,32,2048]{3,1,0,2:T(8,128)(2,1)}), bf16[1,32,4,2048]{3,1,0,2:T(8,128)(2,1)}) %reduce-scatter.4.cloned.1.call-update) | async-done | bytes 524304 | tf_op jit(solution)/shard_map/reduce_scatter | solution.py:181
  476.4 1.1 convert_element_type.131
  (132 shorter events, 31.9 us)
Async XLA Ops:
  7.2 5.2 %copy-start.27 = (bf16[1,32,4,1024]{3,2,1,0:T(4,128)(2,1)S(1)}, bf16[1,32,4,1024]{3,2,1,0:T(4,128)(2,1)}, u32[]{:S(2)}) copy-start(bf16[1,32,4,1024]{3,2,1,0:T(4,128)(2,1)} %param.12) | copy-start | bytes 786436
  7.2 6.1 %copy-start.31 = (bf16[128,32]{0,1:T(8,128)(2,1)S(1)}, bf16[128,32]{0,1:T(8,128)(2,1)}, u32[]{:S(2)}) copy-start(bf16[128,32]{0,1:T(8,128)(2,1)} %param.17) | copy-start | bytes 24580
  7.2 56.2 %copy-start.30 = (bf16[3,32,128]{2,1,0:T(8,128)(2,1)S(1)}, bf16[3,32,128]{2,1,0:T(8,128)(2,1)}, u32[]{:S(2)}) copy-start(bf16[3,32,128]{2,1,0:T(8,128)(2,1)} %param.16) | copy-start | bytes 73732
  7.2 98.0 %all-gather.3.cloned.1.call-start = ((), (), s32[]{:S(2)}) async-start(), calls=%async_computation.3 | async-start | bytes 2359296 | tf_op jit(solution)/shard_map/all_gather | solution.py:125
  12.2 92.9 %copy-start.32 = (f32[16]{0:T(128)S(1)}, f32[16]{0:T(128)}, u32[]{:S(2)}) copy-start(f32[16]{0:T(128)} %param.15) | copy-start | bytes 196
  12.3 116.0 %all-gather.5.cloned.1.call-start = ((), (), s32[]{:S(2)}) async-start(), calls=%async_computation.4 | async-start | bytes 2359296 | tf_op jit(solution)/shard_map/all_gather | solution.py:126
  13.2 247.2 %reduce-scatter.8.cloned.1.call-start = ((), (), s32[]{:S(2)}) async-start(), calls=%async_computation.7 | async-start | bytes 270336 | tf_op jit(solution)/shard_map/reduce_scatter | solution.py:170
  108.0 6.2 %copy-start.3 = (bf16[1,32,32,1024]{3,2,1,0:T(8,128)(2,1)}, bf16[1,32,32,1024]{3,2,1,0:T(8,128)(2,1)S(1)}, u32[]{:S(2)}) copy-start(bf16[1,32,32,1024]{3,2,1,0:T(8,128)(2,1)S(1)} %copy.38) | copy-start | bytes 6291460
  110.6 3.7 copy-start.29
  114.2 1.1 copy-start.14
  128.3 2.8 copy-start.1
  128.3 2.8 copy-start.20
  131.1 2.6 copy-start.5
  138.0 1.2 copy-start.7
  144.5 1.2 copy-start.7
  146.8 3.3 copy-start.9
  146.8 4.1 copy-start.19
  150.0 2.5 copy-start.21
  152.5 2.1 copy-start.15
  154.5 1.9 copy-start.4
  154.6 222.2 %reduce-scatter.6.cloned.1.call-start = ((), (), s32[]{:S(2)}) async-start(), calls=%async_computation.6 | async-start | bytes 811008 | tf_op jit(solution)/shard_map/reduce_scatter | solution.py:167
  156.5 1.1 copy-start.17
  156.5 1.3 copy-start.22
  157.9 1.0 copy-start.23
  157.9 2.1 copy-start.13
  160.0 3.9 copy-start.26
  163.6 1.2 copy-start.10
  163.6 312.8 %reduce-scatter.4.cloned.1.call-start = ((), (), s32[]{:S(2)}) async-start(), calls=%async_computation.5 | async-start | bytes 4718592 | tf_op jit(solution)/shard_map/reduce_scatter | solution.py:181
  163.9 2.3 copy-start.2
  166.2 1.6 copy-start.11
  183.3 294.3 %copy-start.18 = (bf16[1,32,4,1024]{3,2,1,0:T(4,128)(2,1)S(1)}, bf16[1,32,4,1024]{3,2,1,0:T(4,128)(2,1)}, u32[]{:S(2)}) copy-start(bf16[1,32,4,1024]{3,2,1,0:T(4,128)(2,1)} %param.11) | copy-start | bytes 786436
  183.3 294.4 %copy-start.28 = (bf16[1,32,4,1024]{3,2,1,0:T(4,128)(2,1)S(1)}, bf16[1,32,4,1024]{3,2,1,0:T(4,128)(2,1)}, u32[]{:S(2)}) copy-start(bf16[1,32,4,1024]{3,2,1,0:T(4,128)(2,1)} %param.12) | copy-start | bytes 786436
  (8 other events, 7.0 us)
Sparse Core Ops, SparseCore 0:
  12.4 59.3 all-gather.2
  73.6 54.6 all-gather.4
  154.7 105.6 reduce-scatter.7
  264.3 112.4 reduce-scatter.5
  379.3 97.0 reduce-scatter.3
where the time goes:
time: 487 us; the launch traced here: 486 us
  waiting for transfers between devices  297 us (61%)
  blocking collectives  89.2 us (18%)
  local copies, waits for them, and re-layouts  39.5 us (8%)
  matrix products  31.1 us (6%)
  between operations  14.9 us (3%)
  other arithmetic  14.2 us (3%)
    reduce_scatter x1, waiting for transfers between devices, per_device(): lax.psum_scatter(local_qkv.astype(jnp.bfloat16), 'rows', scatter_dimensio...  115 us
    reduce_scatter x1, waiting for transfers between devices, per_device(): lax.psum_scatter(terms.astype(jnp.bfloat16), 'cols', scatter_dimension=2,...  98.3 us
    reduce_scatter x1, waiting for transfers between devices, per_device(): lax.psum_scatter(local_out.astype(jnp.bfloat16), 'rows', scatter_dimensio...  77.1 us
    all_gather x1, blocking collectives, per_device(): lax.all_gather(w_out, 'rows', axis=1, tiled=True)  50.1 us
    all_gather x1, blocking collectives, per_device(): lax.all_gather(w_qkv, 'rows', axis=1, tiled=True)  39.1 us
    unnamed x66, local copies, waits for them, and re-layouts  10.1 us
  transfers between devices with their start and end apart: 5, of which 4 were waited for; matrix products, arithmetic and copies ran while one was open for 9% of the time, Pallas kernels for 0%

commit v1 on v0

v1 whole, which is shorter than its diff:
```python
import jax
import jax.numpy as jnp
from jax import lax
from jax.experimental import pallas as pl
from jax.experimental.pallas import tpu as pltpu
from jax.sharding import PartitionSpec as P

EPS = 1e-06
LOG2E = 1.4426950408889634
MESH = pl.DeviceIdType.MESH
F32 = jnp.float32
BF16 = jnp.bfloat16
NSEM = 180
OWN = {(0, 128): (256, 384), (0, 256): (0, 256), (256, 384): (384, 512)}


def dot(a, b):
    return jnp.dot(a, b, preferred_element_type=F32)


def dot_nt(a, b):
    return lax.dot_general(a, b, (((1,), (1,)), ((), ())), preferred_element_type=F32)


def kernel(
    hs_ref, x_ref, g_ref, gain_ref, wqkv_ref, wout_ref,
    out_ref, gtok_ref, gqkv_ref, gout_ref,
    xs, n_all, g_two, n_t, wa, wb, wc,
    u_t, r_t, kq_t, kz, kq, v_x, v_t, p_all, attn, inv, ext, da_send, da_in,
    go_f, go_send, go_half, go_in,
    dk_t, dq_t, gp, a_in, g_in, part_own, part_send, part_in,
    gw_f, gw_b, gw_sib, gw_sum, gw_in, held,
    send_sem, recv_sem,
):
    r = lax.axis_index("rows")
    c = lax.axis_index("cols")
    y, xl = c // 2, c % 2
    xh, z, core = r // 16, (r // 2) % 8, r % 2
    m16 = r // 2

    def at_cols(yy, xx):
        return {"rows": r, "cols": yy * 2 + xx}

    def at_rows(xx, zz, cc):
        return {"rows": (xx * 8 + zz) * 2 + cc, "cols": c}

    yp, ym, yf = (y + 1) % 4, (y + 3) % 4, (y + 2) % 4
    up, down, side = at_cols(yp, xl), at_cols(ym, xl), at_cols(y, 1 - xl)
    zup, zdown = at_rows(xh, (z + 1) % 8, core), at_rows(xh, (z + 7) % 8, core)
    sib, over = at_rows(xh, z, 1 - core), at_rows(1 - xh, z, core)

    sends = []
    count = [0]

    def copy_of(k, src, dst, dev):
        return pltpu.make_async_remote_copy(
            src_ref=src, dst_ref=dst, send_sem=send_sem.at[k], recv_sem=recv_sem.at[k],
            device_id=dev, device_id_type=MESH,
        )

    def push(src, dst, dev):
        k = count[0]
        count[0] += 1
        d = copy_of(k, src, dst, dev)
        d.start()
        sends.append(d)
        return k

    def send(ref, dev):
        return push(ref, ref, dev)

    def arrive(k, ref):
        copy_of(k, ref, ref, side).wait_recv()

    barrier = pltpu.get_barrier_semaphore()
    peers = [at_cols((y + i) % 4, xl) for i in (1, 2, 3)]
    peers += [side, sib]
    peers += [{"rows": ((m16 + i) % 16) * 2 + core, "cols": c} for i in range(1, 16)]
    for dev in peers:
        pl.semaphore_signal(barrier, inc=1, device_id=dev, device_id_type=MESH)

    xf = x_ref[0].astype(F32).reshape(128, 1024)
    xs[...] = xf
    rs = lax.rsqrt(jnp.mean(xf * xf, -1, keepdims=True) + EPS)
    gain = gain_ref[...]
    n_all[c] = (xf * rs * gain).astype(BF16).reshape(2, 4, 16, 1024)
    g_two[xl] = g_ref[0].astype(F32).reshape(128, 1024).astype(BF16)
    wq, wk = wqkv_ref[0], wqkv_ref[1]
    wa[0, xh, z, core] = jnp.concatenate(
        [wqkv_ref[2], wk[:, :64], wq[:, :64], wout_ref[...], wk[:, 64:], wq[:, 64:]], -1
    )
    kz[...] = jnp.zeros_like(kz)
    pl.semaphore_wait(barrier, len(peers))

    k_over = send(wa.at[0, xh, z, core], over)

    def to_rows(buf, x_from, other, pieces):
        keys = []
        for i in (1, 2, 3):
            for src, dst in pieces:
                k = push(
                    wa.at[0, x_from, z, core, :, src[0]:src[1]],
                    buf.at[3 - i, x_from, z, core, :, dst[0]:dst[1]],
                    at_cols((y + i) % 4, xl),
                )
                keys.append((k, buf.at[3 - i, (xh + other) % 2, z, core, :, dst[0]:dst[1]]))
        return keys

    def come(keys):
        for k, ref in keys:
            arrive(k, ref)

    out_piece = [((256, 384), (0, 128))]
    qkv_pieces = [((0, 256), (0, 256)), ((384, 512), (256, 384))]
    b_keys = to_rows(wb, xh, 0, out_piece)

    def slot(yy, xx):
        return yy * 2 + xx

    def stage_two(buf, ks):
        k_side, k_up, k_down = ks
        below, above, next_to = slot(ym, xl), slot(yp, xl), slot(y, 1 - xl)
        arrive(k_up, buf.at[below])
        b0 = send(buf.at[below, 0], up)
        b1 = send(buf.at[below, :, 3], side)
        arrive(k_down, buf.at[above])
        a0 = send(buf.at[above, 1], down)
        a1 = send(buf.at[above, :, 3], side)
        arrive(k_side, buf.at[next_to])
        s0 = send(buf.at[next_to, :, 0:3], up)
        s1 = send(buf.at[next_to, :, 0:3], down)
        return b0, b1, a0, a1, s0, s1

    def stage_three(buf, ks):
        b0, b1, a0, a1, s0, s1 = ks
        far, below, above = slot(yf, xl), slot(ym, 1 - xl), slot(yp, 1 - xl)
        arrive(b0, buf.at[far, 0])
        f0 = send(buf.at[far, 0, 3], side)
        arrive(a0, buf.at[far, 1])
        f1 = send(buf.at[far, 1, 3], side)
        arrive(s0, buf.at[below, :, 0:3])
        e0 = send(buf.at[below, 0, 0:3], up)
        arrive(s1, buf.at[above, :, 0:3])
        e1 = send(buf.at[above, 1, 0:3], down)
        return b1, a1, f0, f1, e0, e1

    def stage_four(buf, ks):
        b1, a1, f0, f1, e0, e1 = ks
        far = slot(yf, 1 - xl)
        arrive(b1, buf.at[slot(ym, 1 - xl), :, 3])
        arrive(a1, buf.at[slot(yp, 1 - xl), :, 3])
        arrive(e0, buf.at[far, 0, 0:3])
        arrive(e1, buf.at[far, 1, 0:3])
        arrive(f0, buf.at[far, 0, 3])
        arrive(f1, buf.at[far, 1, 3])

    def turned(yy):
        def one(j, carry):
            s = 2 * yy + j
            n_t[:, pl.ds(pl.multiple_of(s * 128, 128), 128)] = n_all[s].reshape(128, 1024).T
            return carry
        lax.fori_loop(0, 2, one, 0)

    n_own = n_all.at[c]
    n_keys = send(n_own, side), send(n_own, up), send(n_own, down)

    class OverZ:
        def __init__(self, buf):
            self.buf = buf
            own = self.block(0)
            self.near = [send(own, self.to(d)) for d in (2, -2, 1, -1)]

        def to(self, d):
            return at_rows(xh, (z + 8 + d) % 8, core)

        def block(self, d):
            return self.buf.at[:, :, (z + 8 + d) % 8, core]

        def half(self, d, h):
            return self.buf.at[:, h, (z + 8 + d) % 8, core]

        def forward(self):
            self.far = []
            for k, d, h in ((self.near[0], -2, 0), (self.near[1], 2, 1)):
                arrive(k, self.block(d))
                one = 1 if d < 0 else -1
                self.far.append(send(self.block(d), self.to(one)))
                self.far.append(send(self.half(d, h), self.to(2 * one)))

        def to_sib(self):
            arrive(self.near[2], self.block(-1))
            arrive(self.near[3], self.block(1))
            arrive(self.far[0], self.block(-3))
            arrive(self.far[2], self.block(3))
            arrive(self.far[1], self.half(4, 0))
            arrive(self.far[3], self.half(4, 1))
            self.k_sib = send(self.buf.at[:, :, :, core], sib)

        def finish(self):
            arrive(self.k_sib, self.buf.at[:, :, :, 1 - core])

    class Ring:
        def __init__(self, buf):
            self.buf = buf
            self.sib_keys = []
            self.up, self.down = send(self.block(z), zup), send(self.block(z), zdown)
            self.to_sib(z)

        def block(self, zz):
            return self.buf.at[:, :, zz, core]

        def half(self, zz, h):
            return self.buf.at[:, h, zz, core]

        def to_sib(self, zz):
            self.sib_keys.append((send(self.block(zz), sib), zz))

        def step(self, d):
            lo, hi = (z + 8 - d) % 8, (z + d) % 8
            arrive(self.up, self.block(lo))
            self.up = send(self.block(lo) if d < 3 else self.half(lo, 0), zup)
            self.to_sib(lo)
            arrive(self.down, self.block(hi))
            self.down = send(self.block(hi) if d < 3 else self.half(hi, 1), zdown)
            self.to_sib(hi)

        def last(self):
            opp = (z + 4) % 8
            arrive(self.up, self.half(opp, 0))
            arrive(self.down, self.half(opp, 1))
            self.to_sib(opp)

        def finish(self):
            for k, zz in self.sib_keys:
                arrive(k, self.buf.at[:, :, zz, 1 - core])

    arrive(k_over, wa.at[0, 1 - xh, z, core])
    za = OverZ(wa)
    b_keys += to_rows(wb, 1 - xh, 1, out_piece)
    come(b_keys)
    zb = OverZ(wb)
    za.forward()
    n_keys = stage_two(n_all, n_keys)
    k_g = send(g_two.at[xl], side)
    zb.forward()
    za.to_sib()
    turned(y)
    n_keys = stage_three(n_all, n_keys)
    zb.to_sib()
    za.finish()

    sc = [hs_ref[c * 2], hs_ref[c * 2 + 1]]
    lane = lax.broadcasted_iota(jnp.int32, (256, 128), 1)
    first = lane < 64
    ones = [
        jnp.where((lane == 64) | (lane == 65), 1.0, 0.0),
        jnp.where(lane < 2, 1.0, 0.0),
    ]

    def rows_of(i):
        return pl.ds(pl.multiple_of(i * 256, 256), 256)

    def project(i):
        rows = rows_of(i)
        n = n_all[pl.ds(2 * i, 2)].reshape(256, 1024)
        w = wa[0].reshape(1024, 512)
        res = dot(n, jnp.concatenate([w[:, :256], w[:, 384:]], -1))
        vv = res[:, :128]
        for h in (0, 1):
            t = res[:, 128 + 128 * h:256 + 128 * h].T.reshape(2, 64, 256)
            rn = lax.rsqrt(jnp.sum(t * t, 1, keepdims=True) + EPS)
            t = t * rn
            u_t[h, :, :, rows] = t
            r_t[h, 0, :, rows] = rn[0]
            r_t[h, 1, :, rows] = rn[1] * sc[h]
            both = jnp.concatenate([t[0], t[1] * (sc[h] * LOG2E)], 0)
            kq_t[h, :, rows] = both.astype(BF16)
            kz[h, 64:128, rows] = t[0].astype(BF16)
            kq[h, rows] = both.T.astype(BF16)
            vx = jnp.where(first if h == 0 else ~first, vv, ones[h]).astype(BF16)
            v_x[h, rows] = vx
            v_t[h, :, rows] = vx.T

    def project_rest(j, carry):
        project((y + j) % 4)
        return carry

    project(y)
    stage_four(n_all, n_keys)
    c_keys = to_rows(wc, xh, 0, qkv_pieces) + to_rows(wc, 1 - xh, 1, qkv_pieces)
    lax.fori_loop(1, 4, project_rest, 0)

    zb.finish()
    arrive(k_g, g_two.at[1 - xl])
    gg = g_two[...].reshape(256, 1024)
    for a in (0, 2):
        w0 = wa[0, :, :, :, :, 256:384] if a == 0 else wb[a - 1]
        w = jnp.concatenate([w0.reshape(1024, 128), wb[a].reshape(1024, 128)], -1)
        t = dot(gg, w).astype(BF16)
        da_send[a] = t[:, :128].reshape(2, 128, 128)
        da_send[a + 1] = t[:, 128:].reshape(2, 128, 128)
    da_keys = []
    for i in (1, 2, 3):
        dst = da_in.at[pl.ds(2 * y, 2)]
        da_keys.append((push(da_send.at[i], dst, at_cols((y + i) % 4, xl)), (y + 4 - i) % 4))
    da_in[pl.ds(2 * y, 2)] = da_send[0]

    lane5 = lax.broadcasted_iota(jnp.int32, (512, 128), 1)

    def forward(i):
        rows = pl.ds(i * 512, 512)
        outs = []
        for h in (0, 1):
            s = dot(kq[h, rows], kz[h])
            p = jnp.exp2(s).astype(BF16)
            p_all[h, rows] = p
            num = dot(p, v_x[h])
            den = num[:, 64:65] if h == 0 else num[:, 0:1]
            iv = (1.0 / den).astype(BF16).astype(F32)
            inv[h, rows] = iv
            outs.append(num * iv)
        attn[pl.ds(4 * i, 4)] = jnp.where(lane5 < 64, outs[0], outs[1]).astype(BF16).reshape(
            4, 128, 128
        )

    forward(0)
    come(c_keys)
    forward(1)

    def spread(buf, into, lo):
        keys = []
        lanes = slice(lo, lo + 128)
        for i in (1, 2, 3):
            to = (y + i) % 4
            src = buf.at[pl.ds(2 * to, 2), :, lanes]
            keys.append((push(src, into.at[4 - i, :, :, lanes], at_cols(to, xl)), 4 - i))
        into[0, :, :, lanes] = buf[pl.ds(2 * y, 2), :, lanes]
        return keys

    def gathered(keys, into, lo):
        for k, rel in keys:
            arrive(k, into.at[rel, :, :, lo:lo + 128])

    a_keys = spread(attn, a_in, 0)
    zc = Ring(wc)
    for j in (1, 2, 3):
        turned((y + j) % 4)

    for k, frm in da_keys:
        arrive(k, da_in.at[pl.ds(2 * frm, 2)])

    def cot(i, carry):
        rows = rows_of(i)
        dd = da_in[pl.ds(2 * i, 2)].reshape(256, 128).astype(F32)
        prod = dd * attn[pl.ds(2 * i, 2)].reshape(256, 128).astype(F32)
        for h in (0, 1):
            iv = inv[h, rows]
            mine = first if h == 0 else ~first
            delta = jnp.sum(jnp.where(mine, prod, 0.0), -1, keepdims=True) * iv
            hi = delta.astype(BF16).astype(F32)
            lo = delta - hi
            at = 64 if h == 0 else 0
            e = jnp.where(mine, dd * iv, jnp.where(lane == at, -hi, jnp.where(lane == at + 1, -lo, 0.0)))
            ext[h, rows] = e.astype(BF16)
        return carry

    lax.fori_loop(0, 4, cot, 0)
    dvs = []
    for h in (0, 1):
        e_t = ext[h].T
        dvs.append(dot(e_t[64 * h:64 * h + 64], p_all[h]))
    gp[:, :, 0:128] = jnp.concatenate(dvs, 0).T.astype(BF16).reshape(8, 128, 128)
    v_keys = spread(gp, g_in, 0)

    def keep_grad(i, res, lo):
        gw_f[pl.ds(4 * i, 4), :, :, lo:lo + 128] = res.reshape(4, 2, 32, 128)
        gw_b[pl.ds(4 * i, 4), :, :, lo:lo + 128] = res.astype(BF16).reshape(4, 2, 32, 128)

    def weight_grad(lo, to):
        def one(i, carry):
            rhs = gp[:, :, lo:lo + 128].reshape(1024, 128)
            keep_grad(i, dot(n_t[rows_of(i), :], rhs), to)
            return carry
        lax.fori_loop(0, 4, one, 0)

    def out_grad_send():
        gg = g_two[...].reshape(256, 1024)
        for i in (2, 1, 3, 0):
            go = dot(a_in[i].reshape(256, 128).T, gg)
            go_f[i] = go
            if i == 2:
                go_send[2] = go.astype(BF16)
                keys = [
                    push(go_send.at[2, 0:64], go_half.at[0], up),
                    push(go_send.at[2, 64:128], go_half.at[1], down),
                ]
        return keys

    def out_grad_on(keys):
        arrive(keys[0], go_half.at[0])
        arrive(keys[1], go_half.at[1])
        go_send[0, 0:64] = (go_f[1, 0:64] + go_half[0].astype(F32)).astype(BF16)
        go_send[0, 64:128] = go_f[1, 64:128].astype(BF16)
        go_send[1, 0:64] = go_f[3, 0:64].astype(BF16)
        go_send[1, 64:128] = (go_f[3, 64:128] + go_half[1].astype(F32)).astype(BF16)
        return push(go_send.at[0], go_in.at[0], up), push(go_send.at[1], go_in.at[1], down)

    def out_grad(keys):
        arrive(keys[0], go_in.at[0])
        arrive(keys[1], go_in.at[1])
        for i in range(4):
            cols = slice(256 * i, 256 * i + 256)
            tot = go_f[0, :, cols] + go_in[0, :, cols].astype(F32) + go_in[1, :, cols].astype(F32)
            keep_grad(i, tot.T, 256)

    def pair_send(lo, hi):
        return push(gw_b.at[:, 1 - core, :, lo:hi], gw_sib.at[:, :, lo:hi], sib)

    def reduce_send(k, lo, hi):
        arrive(k, gw_sib.at[:, :, lo:hi])
        tot = gw_f[:, core, :, lo:hi] + gw_sib[:, :, lo:hi].astype(F32)
        gw_f[:, core, :, lo:hi] = tot
        gw_sum[:, :, lo:hi] = tot.astype(BF16)
        keys = []
        for i in range(1, 16):
            to = (m16 + i) % 16
            dev = {"rows": to * 2 + core, "cols": c}
            keys.append(
                (push(gw_sum.at[to, :, lo:hi], gw_in.at[m16, :, lo:hi], dev), (m16 + 16 - i) % 16)
            )
        return keys

    def reduce_done(keys, lo, hi):
        tot = gw_f[m16, core, :, lo:hi]
        for k, frm in keys:
            arrive(k, gw_in.at[frm, :, lo:hi])
            tot = tot + gw_in[frm, :, lo:hi].astype(F32)
        return tot

    def terms(into, nb, lo, hi, own, others):
        acc = None
        parts = slice(4 * (nb % 2), 4 * (nb % 2) + 4)
        for yy in range(4):
            a = jnp.concatenate([into[yy, 1 - xl, :, lo:hi], into[yy, xl, :, lo:hi]], 0)
            rows = (nb // 2, parts)
            if yy:
                w = others[yy - 1, rows[0], rows[1], :, :, lo:hi].reshape(256, hi - lo)
            else:
                p, q = OWN[lo, hi]
                w = own[0, rows[0], rows[1], :, :, p:q].reshape(256, q - p)
            t = dot_nt(a, w)
            acc = t if acc is None else acc + t
        return acc

    gathered(a_keys, a_in, 0)
    go_keys = out_grad_send()
    for nb in range(4):
        acc = terms(a_in, nb, 0, 128, wa, wb)
        part_send[0, nb] = acc[:128].astype(BF16)
        part_own[0, :, 256 * nb:256 * nb + 256] = acc[128:]
    k_out = push(part_send.at[0], part_in.at[0], side)
    zc.step(1)
    weight_grad(0, 0)

    def backward_head(h, between=None):
        dk_t[...] = jnp.zeros_like(dk_t)

        def one(i, carry):
            rows = pl.ds(i * 512, 512)
            dpd = dot(ext[h, rows], v_t[h])
            ds = (p_all[h, rows].astype(F32) * dpd).astype(BF16)
            dq_t[:, rows] = dot(ds, kq[h]).T[:64]
            dk_t[...] += dot(kq_t[h, 64:128, rows], ds)
            return carry

        one(0, 0)
        got = between() if between else None
        one(1, 0)

        def maps(i, carry):
            rows = rows_of(i)
            d = jnp.stack([dk_t[:, rows] * (1.0 / LOG2E), dq_t[:, rows]])
            u = u_t[h, :, :, rows]
            d = r_t[h, :, :, rows] * (d - u * jnp.sum(u * d, 1, keepdims=True))
            gp[pl.ds(2 * i, 2), :, 128 + 128 * h:256 + 128 * h] = (
                d.reshape(128, 256).T.astype(BF16).reshape(2, 128, 128)
            )
            return carry

        lax.fori_loop(0, 4, maps, 0)
        return got

    backward_head(0)
    h0_keys = spread(gp, g_in, 128)
    zc.step(2)
    go_keys = out_grad_on(go_keys)
    weight_grad(128, 128)
    k_pair0 = pair_send(0, 256)

    def meanwhile():
        zc.step(3)
        return reduce_send(k_pair0, 0, 256)

    rs0 = backward_head(1, meanwhile)
    h1_keys = spread(gp, g_in, 256)
    zc.last()
    weight_grad(256, 384)
    out_grad(go_keys)
    k_pair1 = pair_send(256, 512)

    gathered(v_keys, g_in, 0)
    gathered(h0_keys, g_in, 128)
    zc.finish()
    for nb in range(4):
        held[nb] = terms(g_in, nb, 0, 256, wa, wc)
    rs1 = reduce_send(k_pair1, 256, 512)
    gathered(h1_keys, g_in, 256)
    back = []
    for nb in range(4):
        acc = held[nb] + terms(g_in, nb, 256, 384, wa, wc)
        part_send[1, nb] = acc[:128].astype(BF16)
        part_own[1, :, 256 * nb:256 * nb + 256] = acc[128:]
        back.append(push(part_send.at[1, nb], part_in.at[1, nb], side))

    def whole(which):
        return jnp.concatenate([part_in[which, nb] for nb in range(4)], -1).astype(F32)

    arrive(k_out, part_in.at[0])
    xf = xs[...]
    out_ref[0] = (xf + part_own[0] + whole(0)).reshape(32, 4, 1024).astype(BF16)
    got = reduce_done(rs0, 0, 256)
    gqkv_ref[2] = got[:, 0:128]
    got0 = got[:, 128:256]
    for nb in range(4):
        arrive(back[nb], part_in.at[1, nb])
    dn = (part_own[1] + whole(1)) * gain
    inner = jnp.mean(xf * dn, -1, keepdims=True)
    rs = lax.rsqrt(jnp.mean(xf * xf, -1, keepdims=True) + EPS)
    gt = g_two[xl].astype(F32) + rs * (dn - xf * (rs * rs * inner))
    gtok_ref[0] = gt.reshape(32, 4, 1024).astype(BF16)
    got1 = reduce_done(rs1, 256, 512)
    gout_ref[...] = got1[:, 0:128]
    got1 = got1[:, 128:256]
    gqkv_ref[0] = jnp.concatenate([got0[:, 64:], got1[:, 64:]], -1)
    gqkv_ref[1] = jnp.concatenate([got0[:, :64], got1[:, :64]], -1)
    for d in sends:
        d.wait_send()
    assert count[0] <= NSEM


def per_device(image_tokens, cotangent, noise_level, cond_table, head_scale, w_qkv, w_out):
    gain = lax.dynamic_slice_in_dim(cond_table, noise_level[0], 1, 0)
    vm = pl.BlockSpec(memory_space=pltpu.VMEM)
    sm = pl.BlockSpec(memory_space=pltpu.SMEM)
    V = pltpu.VMEM
    out, gtok, gqkv, gout = pl.pallas_call(
        kernel,
        out_shape=(
            jax.ShapeDtypeStruct((1, 32, 4, 1024), BF16),
            jax.ShapeDtypeStruct((1, 32, 4, 1024), BF16),
            jax.ShapeDtypeStruct((3, 32, 128), F32),
            jax.ShapeDtypeStruct((32, 128), F32),
        ),
        in_specs=[sm, vm, vm, vm, vm, vm],
        out_specs=[vm, vm, vm, vm],
        scratch_shapes=[
            V((128, 1024), F32),
            V((8, 2, 4, 16, 1024), BF16),
            V((2, 128, 1024), BF16),
            V((1024, 1024), BF16),
            V((1, 2, 8, 2, 32, 512), BF16),
            V((3, 2, 8, 2, 32, 128), BF16),
            V((3, 2, 8, 2, 32, 384), BF16),
            V((2, 2, 64, 1024), F32),
            V((2, 2, 1, 1024), F32),
            V((2, 128, 1024), BF16),
            V((2, 128, 1024), BF16),
            V((2, 1024, 128), BF16),
            V((2, 1024, 128), BF16),
            V((2, 128, 1024), BF16),
            V((2, 1024, 1024), BF16),
            V((8, 128, 128), BF16),
            V((2, 1024, 1), F32),
            V((2, 1024, 128), BF16),
            V((4, 2, 128, 128), BF16),
            V((8, 128, 128), BF16),
            V((4, 128, 1024), F32),
            V((3, 128, 1024), BF16),
            V((2, 64, 1024), BF16),
            V((2, 128, 1024), BF16),
            V((64, 1024), F32),
            V((64, 1024), F32),
            V((8, 128, 384), BF16),
            V((4, 2, 128, 128), BF16),
            V((4, 2, 128, 384), BF16),
            V((2, 128, 1024), F32),
            V((2, 4, 128, 256), BF16),
            V((2, 4, 128, 256), BF16),
            V((16, 2, 32, 512), F32),
            V((16, 2, 32, 512), BF16),
            V((16, 32, 512), BF16),
            V((16, 32, 512), BF16),
            V((16, 32, 512), BF16),
            V((4, 256, 256), F32),
            pltpu.SemaphoreType.DMA((NSEM,)),
            pltpu.SemaphoreType.DMA((NSEM,)),
        ],
        compiler_params=pltpu.CompilerParams(
            collective_id=0, has_side_effects=True, vmem_limit_bytes=56 * 1024 * 1024
        ),
        cost_estimate=pl.CostEstimate(
            flops=4_800_000_000, bytes_accessed=4_000_000, transcendentals=2_200_000
        ),
    )(head_scale, image_tokens, cotangent, gain, w_qkv, w_out.T)
    return out, gtok, gqkv, gout.T


def solution(mesh):
    return jax.shard_map(
        per_device,
        mesh=mesh,
        in_specs=(
            P("rows", None, "cols", None),
            P("rows", None, "cols", None),
            P("rows"),
            P(),
            P(),
            P(None, "rows", "cols"),
            P("cols", "rows"),
        ),
        out_specs=(
            P("rows", None, "cols", None),
            P("rows", None, "cols", None),
            P(None, "rows", "cols"),
            P("cols", "rows"),
        ),
        check_vma=False,
    )
```

time: 487 us -> 86.1 us (0.18)
  waiting for transfers between devices: 297 us -> 0 us
  blocking collectives: 89.2 us -> 0 us
  Pallas kernels: 0 us -> 79.4 us
  local copies, waits for them, and re-layouts: 39.5 us -> 5.01 us
  matrix products: 31.1 us -> 0 us
  other arithmetic: 14.2 us -> 0 us
  between operations: 14.9 us -> 1.4 us
    reduce_scatter x3 -> x0, waiting for transfers between devices: 290 us -> none  [the longest x1 115 us: per_device(): lax.psum_scatter(local_qkv.astype(jnp.bfloat16), 'rows', scatter_dimensio...]
    all_gather x2 -> x0, blocking collectives: 89.2 us -> none  [the longest x1 50.1 us: per_device(): lax.all_gather(w_out, 'rows', axis=1, tiled=True)]
    pallas_call x0 -> x1, Pallas kernels: none -> 79.4 us  [per_device(): pl.pallas_call(kernel, out_shape=(jax.ShapeDtypeStruct((1, 32, 4, 1024),...]
    dot_general x26 -> x0, matrix products: 31.1 us -> none  [the longest x3 4.77 us: per_device(): jnp.dot(normed.T, gp, preferred_element_type=jnp.float32)]
    convert_element_type x10 -> x0, other arithmetic: 7.77 us -> none  [the longest x2 2.66 us: per_device(): grad_w_qkv, grad_w_out = (lax.psum_scatter(local_qkv.astype(jnp.bfloat16)...]
    concatenate x1 -> x0, local copies, waits for them, and re-layouts: 6.62 us -> none  [per_device(): jnp.concatenate([out_term, back_term], -1)]
    convert_element_type x1 -> x0, local copies, waits for them, and re-layouts: 6.46 us -> none  [per_device(): terms.astype(jnp.bfloat16)]
    all_gather x2 -> x0, waiting for transfers between devices: 6.23 us -> none  [the longest x1 6.23 us: per_device(): lax.all_gather(cotangent, 'cols', axis=2, tiled=True)]
  transfers between devices with their start and end apart: 5 -> 0, of which waited for: 4 -> 0; matrix products, arithmetic and copies ran while one was open for 9% -> 0% of each run, Pallas kernels for 0% -> 0%
where the time goes in v1:
time: 86.1 us; the launch traced here: 85.8 us
  Pallas kernels  79.4 us (92%)
  local copies, waits for them, and re-layouts  5.01 us (6%)
  between operations  1.4 us (2%)
    pallas_call x1, Pallas kernels, per_device(): pl.pallas_call(kernel, out_shape=(jax.ShapeDtypeStruct((1, 32, 4, 1024),...  79.4 us
    unnamed x12, local copies, waits for them, and re-layouts  4.41 us

profile of v1, /device:TPU:1, one launch (start us, length us, event | category | flops | bytes accessed | tf_op | source)
XLA Modules:
  0.0 85.8 jit_solution(2167915501055556221)
XLA Ops:
  0.6 0.0 copy-start
  1.4 0.5 copy-done
  1.9 0.6 constant_dynamic-slice_fusion.gain_ref
  2.5 79.4 %shard_map.102 = (bf16[1,32,4,1024]{3,2,1,0:T(4,128)(2,1)}, bf16[1,32,4,1024]{3,2,1,0:T(4,128)(2,1)}, f32[3,32,128]{2,1,0:T(8,128)}, f32[32,128]{1,0:T(8,128)}) custom-call(f32[16]{0:T(128)} %hs_ref.1, bf16[1,32,4,1024]{3,2,1,0:T(4,128)(2,1)} %x_ref.1, bf16[1,32,4,1024]{3,2,1,0:T(4,128)(2,1)} %g_ref.1, f32[1,1024]{1,0:T(1,128)} %constant_dynamic-slice_fusion.gain_ref, ...), custom_call_target="tpu_custom_call" | custom-call | flops 4800000000 | bytes 4000000 | tf_op jit(solution)/shard_map/pallas_call | solution.py:556
  81.9 0.0 copy-start.1
  81.9 1.8 %copy.16 = bf16[1,32,4,1024]{3,2,1,0:T(4,128)(2,1)} copy(bf16[1,32,4,1024]{3,2,1,0:T(4,128)(2,1)} %get-tuple-element.16) | data formatting | bytes 524288
  83.7 0.0 copy-done.1
  83.7 0.0 copy-start.2
  83.7 0.7 copy.17
  84.4 0.1 copy-done.2
  84.5 0.0 copy-start.3
  84.5 0.6 copy.18
  85.1 0.1 copy-done.3
  85.2 0.6 copy.19
Async XLA Ops:
  0.6 1.2 %copy-start = (f32[256,1024]{1,0:T(8,128)S(1)}, f32[256,1024]{1,0:T(8,128)}, u32[]{:S(2)}) copy-start(f32[256,1024]{1,0:T(8,128)} %param.10) | copy-start | bytes 3145732
  81.9 1.8 %copy-start.1 = (bf16[1,32,4,1024]{3,2,1,0:T(4,128)(2,1)S(1)}, bf16[1,32,4,1024]{3,2,1,0:T(4,128)(2,1)}, u32[]{:S(2)}) copy-start(bf16[1,32,4,1024]{3,2,1,0:T(4,128)(2,1)} %get-tuple-element.17) | copy-start | bytes 786436
  83.7 0.8 copy-start.2
  84.5 0.7 copy-start.3

commit v2 on v1

--- a/solution.py
+++ b/solution.py
@@ -23,14 +23,14 @@
 
 
 def kernel(
-    hs_ref, x_ref, g_ref, gain_ref, wqkv_ref, wout_ref,
+    lvl_ref, hs_ref, x_hbm, g_hbm, cond_hbm, wqkv_ref, wout_ref,
     out_ref, gtok_ref, gqkv_ref, gout_ref,
     xs, n_all, g_two, n_t, wa, wb, wc,
     u_t, r_t, kq_t, kz, kq, v_x, v_t, p_all, attn, inv, ext, da_send, da_in,
-    go_f, go_send, go_half, go_in,
+    g_t, go_f, go_b, go_sib, go_send, go_half, go_in,
     dk_t, dq_t, gp, a_in, g_in, part_own, part_send, part_in,
     gw_f, gw_b, gw_sib, gw_sum, gw_in, held,
-    send_sem, recv_sem,
+    x_ref, g_ref, cond_ref, send_sem, recv_sem, in_sem,
 ):
     r = lax.axis_index("rows")
     c = lax.axis_index("cols")
@@ -79,17 +79,28 @@
     for dev in peers:
         pl.semaphore_signal(barrier, inc=1, device_id=dev, device_id_type=MESH)
 
-    xf = x_ref[0].astype(F32).reshape(128, 1024)
-    xs[...] = xf
-    rs = lax.rsqrt(jnp.mean(xf * xf, -1, keepdims=True) + EPS)
-    gain = gain_ref[...]
-    n_all[c] = (xf * rs * gain).astype(BF16).reshape(2, 4, 16, 1024)
-    g_two[xl] = g_ref[0].astype(F32).reshape(128, 1024).astype(BF16)
+    fetch = [
+        pltpu.make_async_copy(src, dst, in_sem.at[i])
+        for i, (src, dst) in enumerate(
+            [(x_hbm.at[0], x_ref), (g_hbm.at[0], g_ref), (cond_hbm, cond_ref)]
+        )
+    ]
+    for f in fetch:
+        f.start()
     wq, wk = wqkv_ref[0], wqkv_ref[1]
     wa[0, xh, z, core] = jnp.concatenate(
         [wqkv_ref[2], wk[:, :64], wq[:, :64], wout_ref[...], wk[:, 64:], wq[:, 64:]], -1
     )
     kz[...] = jnp.zeros_like(kz)
+    fetch[0].wait()
+    xf = x_ref[...].astype(F32).reshape(128, 1024)
+    xs[...] = xf
+    rs = lax.rsqrt(jnp.mean(xf * xf, -1, keepdims=True) + EPS)
+    fetch[2].wait()
+    gain = cond_ref[pl.ds(lvl_ref[0], 1), :]
+    n_all[c] = (xf * rs * gain).astype(BF16).reshape(2, 4, 16, 1024)
+    fetch[1].wait()
+    g_two[xl] = g_ref[...].astype(F32).reshape(128, 1024).astype(BF16)
     pl.semaphore_wait(barrier, len(peers))
 
     k_over = send(wa.at[0, xh, z, core], over)
@@ -144,11 +155,13 @@
         e1 = send(buf.at[above, 1, 0:3], down)
         return b1, a1, f0, f1, e0, e1
 
-    def stage_four(buf, ks):
-        b1, a1, f0, f1, e0, e1 = ks
+    def near_done(buf, ks):
+        arrive(ks[0], buf.at[slot(ym, 1 - xl), :, 3])
+        arrive(ks[1], buf.at[slot(yp, 1 - xl), :, 3])
+
+    def far_done(buf, ks):
+        f0, f1, e0, e1 = ks[2:]
         far = slot(yf, 1 - xl)
-        arrive(b1, buf.at[slot(ym, 1 - xl), :, 3])
-        arrive(a1, buf.at[slot(yp, 1 - xl), :, 3])
         arrive(e0, buf.at[far, 0, 0:3])
         arrive(e1, buf.at[far, 1, 0:3])
         arrive(f0, buf.at[far, 0, 3])
@@ -237,16 +250,15 @@
     arrive(k_over, wa.at[0, 1 - xh, z, core])
     za = OverZ(wa)
     b_keys += to_rows(wb, 1 - xh, 1, out_piece)
+    za.forward()
     come(b_keys)
     zb = OverZ(wb)
-    za.forward()
     n_keys = stage_two(n_all, n_keys)
     k_g = send(g_two.at[xl], side)
+    za.to_sib()
     zb.forward()
-    za.to_sib()
     turned(y)
     n_keys = stage_three(n_all, n_keys)
-    zb.to_sib()
     za.finish()
 
     sc = [hs_ref[c * 2], hs_ref[c * 2 + 1]]
@@ -281,18 +293,24 @@
             v_x[h, rows] = vx
             v_t[h, :, rows] = vx.T
 
-    def project_rest(j, carry):
-        project((y + j) % 4)
+    def project_near(j, carry):
+        yy = (y + 1 + 2 * j) % 4
+        project(yy)
+        turned(yy)
         return carry
 
     project(y)
-    stage_four(n_all, n_keys)
+    near_done(n_all, n_keys)
     c_keys = to_rows(wc, xh, 0, qkv_pieces) + to_rows(wc, 1 - xh, 1, qkv_pieces)
-    lax.fori_loop(1, 4, project_rest, 0)
+    zb.to_sib()
+    lax.fori_loop(0, 2, project_near, 0)
+    far_done(n_all, n_keys)
+    project(yf)
 
     zb.finish()
     arrive(k_g, g_two.at[1 - xl])
     gg = g_two[...].reshape(256, 1024)
+    g_t[...] = gg.T
     for a in (0, 2):
         w0 = wa[0, :, :, :, :, 256:384] if a == 0 else wb[a - 1]
         w = jnp.concatenate([w0.reshape(1024, 128), wb[a].reshape(1024, 128)], -1)
@@ -304,6 +322,8 @@
         dst = da_in.at[pl.ds(2 * y, 2)]
         da_keys.append((push(da_send.at[i], dst, at_cols((y + i) % 4, xl)), (y + 4 - i) % 4))
     da_in[pl.ds(2 * y, 2)] = da_send[0]
+    come(c_keys)
+    zc = Ring(wc)
 
     lane5 = lax.broadcasted_iota(jnp.int32, (512, 128), 1)
 
@@ -324,13 +344,12 @@
         )
 
     forward(0)
-    come(c_keys)
     forward(1)
 
     def spread(buf, into, lo):
         keys = []
         lanes = slice(lo, lo + 128)
-        for i in (1, 2, 3):
+        for i in (2, 1, 3):
             to = (y + i) % 4
             src = buf.at[pl.ds(2 * to, 2), :, lanes]
             keys.append((push(src, into.at[4 - i, :, :, lanes], at_cols(to, xl)), 4 - i))
@@ -342,9 +361,8 @@
             arrive(k, into.at[rel, :, :, lo:lo + 128])
 
     a_keys = spread(attn, a_in, 0)
-    zc = Ring(wc)
-    for j in (1, 2, 3):
-        turned((y + j) % 4)
+    zc.step(1)
+    turned(yf)
 
     for k, frm in da_keys:
         arrive(k, da_in.at[pl.ds(2 * frm, 2)])
@@ -371,63 +389,64 @@
         dvs.append(dot(e_t[64 * h:64 * h + 64], p_all[h]))
     gp[:, :, 0:128] = jnp.concatenate(dvs, 0).T.astype(BF16).reshape(8, 128, 128)
     v_keys = spread(gp, g_in, 0)
-
-    def keep_grad(i, res, lo):
-        gw_f[pl.ds(4 * i, 4), :, :, lo:lo + 128] = res.reshape(4, 2, 32, 128)
-        gw_b[pl.ds(4 * i, 4), :, :, lo:lo + 128] = res.astype(BF16).reshape(4, 2, 32, 128)
+    zc.step(2)
 
     def weight_grad(lo, to):
-        def one(i, carry):
-            rhs = gp[:, :, lo:lo + 128].reshape(1024, 128)
-            keep_grad(i, dot(n_t[rows_of(i), :], rhs), to)
-            return carry
-        lax.fori_loop(0, 4, one, 0)
+        res = dot(n_t[...], gp[:, :, lo:lo + 128].reshape(1024, 128))
+        gw_f[:, :, :, to:to + 128] = res.reshape(16, 2, 32, 128)
+        gw_b[:, :, :, to:to + 128] = res.astype(BF16).reshape(16, 2, 32, 128)
 
     def out_grad_send():
-        gg = g_two[...].reshape(256, 1024)
-        for i in (2, 1, 3, 0):
-            go = dot(a_in[i].reshape(256, 128).T, gg)
+        for i in range(4):
+            go = dot(g_t[...], a_in[i].reshape(256, 128)).reshape(16, 2, 32, 128)
             go_f[i] = go
-            if i == 2:
-                go_send[2] = go.astype(BF16)
-                keys = [
-                    push(go_send.at[2, 0:64], go_half.at[0], up),
-                    push(go_send.at[2, 64:128], go_half.at[1], down),
-                ]
-        return keys
+            go_b[i] = go.astype(BF16)
+        return push(go_b.at[:, :, 1 - core], go_sib, sib)
+
+    def out_far_send(k):
+        arrive(k, go_sib)
+        for i in range(4):
+            go_f[i, :, core] = go_f[i, :, core] + go_sib[i].astype(F32)
+        go_send[2] = go_f[2, :, core].astype(BF16)
+        return (
+            push(go_send.at[2, 0:8], go_half.at[0], up),
+            push(go_send.at[2, 8:16], go_half.at[1], down),
+        )
 
     def out_grad_on(keys):
         arrive(keys[0], go_half.at[0])
         arrive(keys[1], go_half.at[1])
-        go_send[0, 0:64] = (go_f[1, 0:64] + go_half[0].astype(F32)).astype(BF16)
-        go_send[0, 64:128] = go_f[1, 64:128].astype(BF16)
-        go_send[1, 0:64] = go_f[3, 0:64].astype(BF16)
-        go_send[1, 64:128] = (go_f[3, 64:128] + go_half[1].astype(F32)).astype(BF16)
+        go_send[0, 0:8] = (go_f[1, 0:8, core] + go_half[0].astype(F32)).astype(BF16)
+        go_send[0, 8:16] = go_f[1, 8:16, core].astype(BF16)
+        go_send[1, 0:8] = go_f[3, 0:8, core].astype(BF16)
+        go_send[1, 8:16] = (go_f[3, 8:16, core] + go_half[1].astype(F32)).astype(BF16)
         return push(go_send.at[0], go_in.at[0], up), push(go_send.at[1], go_in.at[1], down)
 
     def out_grad(keys):
         arrive(keys[0], go_in.at[0])
         arrive(keys[1], go_in.at[1])
-        for i in range(4):
-            cols = slice(256 * i, 256 * i + 256)
-            tot = go_f[0, :, cols] + go_in[0, :, cols].astype(F32) + go_in[1, :, cols].astype(F32)
-            keep_grad(i, tot.T, 256)
+        tot = go_f[0, :, core] + go_in[0].astype(F32) + go_in[1].astype(F32)
+        gw_f[:, core, :, 256:384] = tot
+        gw_sum[:, :, 256:384] = tot.astype(BF16)
 
     def pair_send(lo, hi):
         return push(gw_b.at[:, 1 - core, :, lo:hi], gw_sib.at[:, :, lo:hi], sib)
 
-    def reduce_send(k, lo, hi):
+    def reduce_send(k, lo, hi, start):
         arrive(k, gw_sib.at[:, :, lo:hi])
         tot = gw_f[:, core, :, lo:hi] + gw_sib[:, :, lo:hi].astype(F32)
         gw_f[:, core, :, lo:hi] = tot
         gw_sum[:, :, lo:hi] = tot.astype(BF16)
         keys = []
-        for i in range(1, 16):
-            to = (m16 + i) % 16
-            dev = {"rows": to * 2 + core, "cols": c}
-            keys.append(
-                (push(gw_sum.at[to, :, lo:hi], gw_in.at[m16, :, lo:hi], dev), (m16 + 16 - i) % 16)
-            )
+        for dz in (4, 3, 5, 2, 6, 1, 7, 0):
+            for dx in (1, 0):
+                if dx or dz:
+                    to = ((xh + dx) % 2) * 8 + (z + dz) % 8
+                    frm = ((xh + dx) % 2) * 8 + (z + 8 - dz) % 8
+                    dev = {"rows": to * 2 + core, "cols": c}
+                    keys.append(
+                        (push(gw_sum.at[to, :, start:hi], gw_in.at[m16, :, start:hi], dev), frm)
+                    )
         return keys
 
     def reduce_done(keys, lo, hi):
@@ -453,14 +472,15 @@
         return acc
 
     gathered(a_keys, a_in, 0)
-    go_keys = out_grad_send()
+    k_go = out_grad_send()
     for nb in range(4):
         acc = terms(a_in, nb, 0, 128, wa, wb)
         part_send[0, nb] = acc[:128].astype(BF16)
         part_own[0, :, 256 * nb:256 * nb + 256] = acc[128:]
     k_out = push(part_send.at[0], part_in.at[0], side)
-    zc.step(1)
+    go_keys = out_far_send(k_go)
     weight_grad(0, 0)
+    zc.step(3)
 
     def backward_head(h, between=None):
         dk_t[...] = jnp.zeros_like(dk_t)
@@ -490,30 +510,27 @@
         lax.fori_loop(0, 4, maps, 0)
         return got
 
-    backward_head(0)
+    go_keys = backward_head(0, lambda: out_grad_on(go_keys))
     h0_keys = spread(gp, g_in, 128)
-    zc.step(2)
-    go_keys = out_grad_on(go_keys)
+    zc.last()
     weight_grad(128, 128)
     k_pair0 = pair_send(0, 256)
 
     def meanwhile():
-        zc.step(3)
-        return reduce_send(k_pair0, 0, 256)
+        return reduce_send(k_pair0, 0, 256, 0)
 
     rs0 = backward_head(1, meanwhile)
     h1_keys = spread(gp, g_in, 256)
-    zc.last()
     weight_grad(256, 384)
+    k_pair1 = pair_send(384, 512)
     out_grad(go_keys)
-    k_pair1 = pair_send(256, 512)
 
     gathered(v_keys, g_in, 0)
     gathered(h0_keys, g_in, 128)
     zc.finish()
     for nb in range(4):
         held[nb] = terms(g_in, nb, 0, 256, wa, wc)
-    rs1 = reduce_send(k_pair1, 256, 512)
+    rs1 = reduce_send(k_pair1, 384, 512, 256)
     gathered(h1_keys, g_in, 256)
     back = []
     for nb in range(4):
@@ -548,8 +565,13 @@
     assert count[0] <= NSEM
 
 
+def hand_on(*refs):
+    for src, dst in zip(refs[:4], refs[4:]):
+        dst[...] = src[...]
+
+
 def per_device(image_tokens, cotangent, noise_level, cond_table, head_scale, w_qkv, w_out):
-    gain = lax.dynamic_slice_in_dim(cond_table, noise_level[0], 1, 0)
+    hbm = pl.BlockSpec(memory_space=pl.ANY)
     vm = pl.BlockSpec(memory_space=pltpu.VMEM)
     sm = pl.BlockSpec(memory_space=pltpu.SMEM)
     V = pltpu.VMEM
@@ -561,7 +583,7 @@
             jax.ShapeDtypeStruct((3, 32, 128), F32),
             jax.ShapeDtypeStruct((32, 128), F32),
         ),
-        in_specs=[sm, vm, vm, vm, vm, vm],
+        in_specs=[sm, sm, hbm, hbm, hbm, vm, vm],
         out_specs=[vm, vm, vm, vm],
         scratch_shapes=[
             V((128, 1024), F32),
@@ -584,10 +606,13 @@
             V((2, 1024, 128), BF16),
             V((4, 2, 128, 128), BF16),
             V((8, 128, 128), BF16),
-            V((4, 128, 1024), F32),
-            V((3, 128, 1024), BF16),
-            V((2, 64, 1024), BF16),
-            V((2, 128, 1024), BF16),
+            V((1024, 256), BF16),
+            V((4, 16, 2, 32, 128), F32),
+            V((4, 16, 2, 32, 128), BF16),
+            V((4, 16, 32, 128), BF16),
+            V((3, 16, 32, 128), BF16),
+            V((2, 8, 32, 128), BF16),
+            V((2, 16, 32, 128), BF16),
             V((64, 1024), F32),
             V((64, 1024), F32),
             V((8, 128, 384), BF16),
@@ -602,8 +627,12 @@
             V((16, 32, 512), BF16),
             V((16, 32, 512), BF16),
             V((4, 256, 256), F32),
+            V((32, 4, 1024), BF16),
+            V((32, 4, 1024), BF16),
+            V((256, 1024), F32),
             pltpu.SemaphoreType.DMA((NSEM,)),
             pltpu.SemaphoreType.DMA((NSEM,)),
+            pltpu.SemaphoreType.DMA((3,)),
         ],
         compiler_params=pltpu.CompilerParams(
             collective_id=0, has_side_effects=True, vmem_limit_bytes=56 * 1024 * 1024
@@ -611,7 +640,14 @@
         cost_estimate=pl.CostEstimate(
             flops=4_800_000_000, bytes_accessed=4_000_000, transcendentals=2_200_000
         ),
-    )(head_scale, image_tokens, cotangent, gain, w_qkv, w_out.T)
+    )(noise_level, head_scale, image_tokens, cotangent, cond_table, w_qkv, w_out.T)
+    got = (out, gtok, gqkv, gout)
+    out, gtok, gqkv, gout = pl.pallas_call(
+        hand_on,
+        out_shape=tuple(jax.ShapeDtypeStruct(a.shape, a.dtype) for a in got),
+        in_specs=[vm] * 4,
+        out_specs=[vm] * 4,
+    )(*got)
     return out, gtok, gqkv, gout.T
 
 

time: 86.1 us -> 81.1 us (0.942)
  local copies, waits for them, and re-layouts: 5.01 us -> 0 us
    unnamed x12 -> x0, local copies, waits for them, and re-layouts: 4.41 us -> none
    pallas_call x0 -> x1, Pallas kernels: none -> 1.85 us  [per_device(): pl.pallas_call(hand_on, out_shape=tuple((jax.ShapeDtypeStruct(a.shape, a....]
    pallas_call x1, Pallas kernels: 79.4 us -> 77.8 us  [per_device(): pl.pallas_call(kernel, out_shape=(jax.ShapeDtypeStruct((1, 32, 4, 1024),...]
where the time goes in v2:
time: 81.1 us; the launch traced here: 80.9 us
  Pallas kernels  79.6 us (98%)
  between operations  1.29 us (2%)
    pallas_call x1, Pallas kernels, per_device(): pl.pallas_call(kernel, out_shape=(jax.ShapeDtypeStruct((1, 32, 4, 1024),...  77.8 us
    pallas_call x1, Pallas kernels, per_device(): pl.pallas_call(hand_on, out_shape=tuple((jax.ShapeDtypeStruct(a.shape, a....  1.85 us

profile of v2, /device:TPU:1, one launch (start us, length us, event | category | flops | bytes accessed | tf_op | source)
XLA Modules:
  0.0 80.9 jit_solution(12699109718713807837)
XLA Ops:
  1.3 77.8 %shard_map.102 = (bf16[1,32,4,1024]{3,2,1,0:T(4,128)(2,1)}, bf16[1,32,4,1024]{3,2,1,0:T(4,128)(2,1)}, f32[3,32,128]{2,1,0:T(8,128)}, f32[32,128]{1,0:T(8,128)}) custom-call(s32[1]{0:T(128)S(6)} %copy.11.lvl_ref, f32[16]{0:T(128)} %hs_ref.1, bf16[1,32,4,1024]{3,2,1,0:T(4,128)(2,1)} %x_hbm.1, bf16[1,32,4,1024]{3,2,1,0:T(4,128)(2,1)} %g_hbm.1, ...), custom_call_target="tpu_custom_call" | custom-call | flops 4800000000 | bytes 4000000 | tf_op jit(solution)/shard_map/pallas_call | solution.py:578
  79.0 1.8 %shard_map.103 = (bf16[1,32,4,1024]{3,2,1,0:T(4,128)(2,1)}, bf16[1,32,4,1024]{3,2,1,0:T(4,128)(2,1)}, f32[3,32,128]{2,1,0:T(8,128)}, f32[32,128]{1,0:T(8,128)}) custom-call(bf16[1,32,4,1024]{3,2,1,0:T(4,128)(2,1)} %get-tuple-element.12.refs_0_, bf16[1,32,4,1024]{3,2,1,0:T(4,128)(2,1)} %get-tuple-element.13.refs_1_, f32[3,32,128]{2,1,0:T(8,128)} %get-tuple-element.14.refs_2_, ...), custom_call_target="tpu_custom_call" | custom-call | tf_op jit(solution)/shard_map/pallas_call | solution.py:645

commit v3 on v2

--- a/solution.py
+++ b/solution.py
@@ -16,10 +16,6 @@
 
 def dot(a, b):
     return jnp.dot(a, b, preferred_element_type=F32)
-
-
-def dot_nt(a, b):
-    return lax.dot_general(a, b, (((1,), (1,)), ((), ())), preferred_element_type=F32)
 
 
 def kernel(
@@ -456,25 +452,31 @@
             tot = tot + gw_in[frm, :, lo:hi].astype(F32)
         return tot
 
-    def terms(into, nb, lo, hi, own, others):
+    def turned_rows(into, lo, hi):
+        return [
+            jnp.concatenate([into[yy, 1 - xl, :, lo:hi], into[yy, xl, :, lo:hi]], 0).T
+            for yy in range(4)
+        ]
+
+    def terms(turned_in, nb, lo, hi, own, others):
         acc = None
         parts = slice(4 * (nb % 2), 4 * (nb % 2) + 4)
         for yy in range(4):
-            a = jnp.concatenate([into[yy, 1 - xl, :, lo:hi], into[yy, xl, :, lo:hi]], 0)
             rows = (nb // 2, parts)
             if yy:
                 w = others[yy - 1, rows[0], rows[1], :, :, lo:hi].reshape(256, hi - lo)
             else:
                 p, q = OWN[lo, hi]
                 w = own[0, rows[0], rows[1], :, :, p:q].reshape(256, q - p)
-            t = dot_nt(a, w)
+            t = dot(w, turned_in[yy])
             acc = t if acc is None else acc + t
         return acc
 
     gathered(a_keys, a_in, 0)
     k_go = out_grad_send()
+    a_turned = turned_rows(a_in, 0, 128)
     for nb in range(4):
-        acc = terms(a_in, nb, 0, 128, wa, wb)
+        acc = terms(a_turned, nb, 0, 128, wa, wb).T
         part_send[0, nb] = acc[:128].astype(BF16)
         part_own[0, :, 256 * nb:256 * nb + 256] = acc[128:]
     k_out = push(part_send.at[0], part_in.at[0], side)
@@ -528,13 +530,15 @@
     gathered(v_keys, g_in, 0)
     gathered(h0_keys, g_in, 128)
     zc.finish()
+    g_turned = turned_rows(g_in, 0, 256)
     for nb in range(4):
-        held[nb] = terms(g_in, nb, 0, 256, wa, wc)
+        held[nb] = terms(g_turned, nb, 0, 256, wa, wc)
     rs1 = reduce_send(k_pair1, 384, 512, 256)
     gathered(h1_keys, g_in, 256)
     back = []
+    g_turned = turned_rows(g_in, 256, 384)
     for nb in range(4):
-        acc = held[nb] + terms(g_in, nb, 256, 384, wa, wc)
+        acc = (held[nb] + terms(g_turned, nb, 256, 384, wa, wc)).T
         part_send[1, nb] = acc[:128].astype(BF16)
         part_own[1, :, 256 * nb:256 * nb + 256] = acc[128:]
         back.append(push(part_send.at[1, nb], part_in.at[1, nb], side))

time: 81.1 us -> 81.4 us (level)
  no operation moved by 1% of the time
where the time goes in v3:
time: 81.4 us; the launch traced here: 81.2 us
  Pallas kernels  79.9 us (98%)
  between operations  1.29 us (2%)
    pallas_call x1, Pallas kernels, per_device(): pl.pallas_call(kernel, out_shape=(jax.ShapeDtypeStruct((1, 32, 4, 1024),...  78.1 us
    pallas_call x1, Pallas kernels, per_device(): pl.pallas_call(hand_on, out_shape=tuple((jax.ShapeDtypeStruct(a.shape, a....  1.85 us

profile of v3, /device:TPU:1, one launch (start us, length us, event | category | flops | bytes accessed | tf_op | source)
XLA Modules:
  0.0 81.2 jit_solution(11973425284794240118)
XLA Ops:
  1.3 78.1 %shard_map.102 = (bf16[1,32,4,1024]{3,2,1,0:T(4,128)(2,1)}, bf16[1,32,4,1024]{3,2,1,0:T(4,128)(2,1)}, f32[3,32,128]{2,1,0:T(8,128)}, f32[32,128]{1,0:T(8,128)}) custom-call(s32[1]{0:T(128)S(6)} %copy.11.lvl_ref, f32[16]{0:T(128)} %hs_ref.1, bf16[1,32,4,1024]{3,2,1,0:T(4,128)(2,1)} %x_hbm.1, bf16[1,32,4,1024]{3,2,1,0:T(4,128)(2,1)} %g_hbm.1, ...), custom_call_target="tpu_custom_call" | custom-call | flops 4800000000 | bytes 4000000 | tf_op jit(solution)/shard_map/pallas_call | solution.py:582
  79.4 1.8 %shard_map.103 = (bf16[1,32,4,1024]{3,2,1,0:T(4,128)(2,1)}, bf16[1,32,4,1024]{3,2,1,0:T(4,128)(2,1)}, f32[3,32,128]{2,1,0:T(8,128)}, f32[32,128]{1,0:T(8,128)}) custom-call(bf16[1,32,4,1024]{3,2,1,0:T(4,128)(2,1)} %get-tuple-element.12.refs_0_, bf16[1,32,4,1024]{3,2,1,0:T(4,128)(2,1)} %get-tuple-element.13.refs_1_, f32[3,32,128]{2,1,0:T(8,128)} %get-tuple-element.14.refs_2_, ...), custom_call_target="tpu_custom_call" | custom-call | tf_op jit(solution)/shard_map/pallas_call | solution.py:649
